TPU v7x, 256 devices: a whole 4x4x8 slice. The times are simulated.
256 devices in a mesh: dp: 16 (over z, core), tensor: 16 (over x, y).
Axes of the slice: x: 4, y: 4, z: 8, core: 2. Of those that a mesh axis runs over, the one named last changes fastest.
Arguments:
- attn_out: bfloat16 [12288, 8192], P('dp', 'tensor'), may hold values from -0.21875 to 0.21875
- grad_out: bfloat16 [12288, 4096], P(('dp', 'tensor')), may hold values from -6 to 6
- weight: bfloat16 [8192, 4096], P('tensor'), may hold values from -0.09375 to 0.09375
- error_feed: bfloat16 [131072, 4096], P(('dp', 'tensor')), may hold values from -6 to 6
- warm_basis: float32 [4096, 64], replicated, may hold values from -0.09375 to 0.09375
Outputs:
- grad_in: bfloat16 [12288, 8192], P('dp', 'tensor')
- new_error: bfloat16 [131072, 4096], P(('dp', 'tensor'))
- new_basis: float32 [4096, 64], replicated
All inputs are finite; a program needn't handle non-finite values.
Results may differ from a plain program's by a relative error of at most 0.013.
Values may be sent and summed in bfloat16 or wider, within the bound.
No kernel may reach another device: no remote copies, remote signals or barrier semaphores. Data moves between devices by JAX's collectives and lax.ppermute only.
A program may use at most 128 MiB of HBM per device.

v0:
```python
import functools

import jax
import jax.numpy as jnp
from jax import lax
from jax.experimental import pallas as pl
from jax.experimental.pallas import tpu as pltpu
from jax.sharding import PartitionSpec as P

F32 = jnp.float32
BF16 = jnp.bfloat16
VMEM = pl.BlockSpec(memory_space=pltpu.VMEM)
MB = 1024 * 1024


def shape(dims, dtype):
    return jax.ShapeDtypeStruct(dims, dtype)


def split_high_low(value):
    high = value.astype(BF16)
    return high, (value - high.astype(F32)).astype(BF16)


def dot(a, b, ca=1, cb=0, precision=None):
    return lax.dot_general(
        a, b, (((ca,), (cb,)), ((), ())), preferred_element_type=F32, precision=precision
    )


def call(kernel, outs, *args, ins=None, out_specs=None, scratch=(), flops=0, moved=0, limit=16, **kw):
    many = isinstance(outs, tuple)
    return pl.pallas_call(
        kernel,
        out_shape=outs,
        in_specs=ins or [VMEM] * len(args),
        out_specs=out_specs or ((VMEM,) * len(outs) if many else VMEM),
        scratch_shapes=list(scratch),
        compiler_params=pltpu.CompilerParams(vmem_limit_bytes=limit * MB),
        cost_estimate=pl.CostEstimate(flops=flops, bytes_accessed=moved, transcendentals=0),
        **kw,
    )(*args)


def core_index():
    return lax.rem(lax.axis_index("dp"), 2)


def store_halves(value, mine_ref, other_ref):
    half = value.shape[1] // 2
    low = core_index() == 0
    left, right = value[:, :half], value[:, half:]
    mine_ref[...] = jnp.where(low, left, right)
    other_ref[...] = jnp.where(low, right, left).astype(other_ref.dtype)


def join_halves(mine, other):
    low = core_index() == 0
    return jnp.concatenate([jnp.where(low, mine, other), jnp.where(low, other, mine)], axis=1)


def token_kernel(cot_hbm, warm_hbm, out_ref, cot_ref, warm_ref, sems):
    rank, width = warm_ref.shape
    chunk = width // 2
    copies = []
    for c in range(2):
        columns = pl.ds(c * chunk, chunk)
        copies.append([
            pltpu.make_async_copy(src.at[:, columns], dst.at[:, columns], sems.at[2 * c + k])
            for k, (src, dst) in enumerate(((warm_hbm, warm_ref), (cot_hbm, cot_ref)))
        ])
    for copy in copies[0] + copies[1]:
        copy.start()
    both = None
    for c in range(2):
        columns = pl.ds(c * chunk, chunk)
        for copy in copies[c]:
            copy.wait()
        warm_2 = jnp.concatenate(split_high_low(warm_ref[:, columns]), axis=0)
        term = dot(cot_ref[:, columns], warm_2, 1, 1)
        both = term if both is None else both + term
    both = jnp.concatenate(split_high_low(both[:, :rank] + both[:, rank:]), axis=1)
    for k in range(out_ref.shape[0]):
        out_ref[k] = both


def part_kernel(q_ref, attn_ref, e_ref, mine_ref, other_ref):
    rank = e_ref.shape[0]
    both = dot(q_ref[...], attn_ref[...], 0, 0)
    store_halves(both[:rank] + both[rank:] + e_ref[...], mine_ref, other_ref)


def spread_kernel(mine_ref, got_ref, out_ref):
    value = (mine_ref[...] + got_ref[...]).astype(BF16)
    for k in range(out_ref.shape[0]):
        out_ref[k] = value


def total_of(ref):
    value = ref[0].astype(F32)
    for k in range(1, ref.shape[0]):
        value = value + ref[k].astype(F32)
    return value


def mean_kernel(replicas, parts_ref, out_ref):
    out_ref[...] = total_of(parts_ref) * (1.0 / replicas)


def feature_kernel(mine_ref, other_ref, attn_ref, panel_ref, out_ref):
    rank = mine_ref.shape[0]
    panel = join_halves(mine_ref[...], other_ref[...])
    panel_ref[...] = panel
    panel_2 = jnp.concatenate(split_high_low(panel), axis=0)
    gram = dot(panel_2, panel_2, 1, 1)
    gram = gram[:rank, :rank] + gram[:rank, rank:] + gram[rank:, :rank] + gram[rank:, rank:]
    part = rank // 2
    gram = jnp.where(core_index() == 0, gram[:part], gram[part:])
    gram = jnp.concatenate(split_high_low(gram), axis=0)
    both = dot(attn_ref[...], panel_2, 1, 1)
    both = (both[:, :rank] + both[:, rank:]).astype(BF16)
    tok = both.shape[0] // out_ref.shape[0]
    for k in range(out_ref.shape[0]):
        out_ref[k, pl.ds(0, tok), pl.ds(0, rank)] = both[k * tok:(k + 1) * tok]
        out_ref[k, pl.ds(tok, rank - tok), pl.ds(0, rank)] = jnp.zeros((rank - tok, rank), BF16)
        out_ref[k, :, pl.ds(rank, rank)] = gram


def error_term_kernel(panel_ref, error_ref, out_ref):
    step = pl.program_id(0)
    rank, rows = panel_ref.shape[0], error_ref.shape[0]
    panel_2 = jnp.concatenate(split_high_low(panel_ref[...]), axis=0)
    for c in range(0, error_ref.shape[1], 1024):
        columns = pl.ds(c, 1024)
        both = dot(panel_2, error_ref[:, columns])
        both = both[:rank] + both[rank:]

        @pl.when(step == 0)
        def _():
            out_ref[:, columns] = both

        @pl.when(step > 0)
        def _():
            out_ref[:, columns] += both


def basis_term_kernel(parts_ref, cot_ref, error_term_ref, mine_ref, other_ref, gram_ref):
    tok, rank = cot_ref.shape[0], error_term_ref.shape[0]
    part = rank // 2
    value = total_of(parts_ref)
    gram_ref[...] = value[:part, rank:] + value[part:, rank:]
    token_2 = jnp.concatenate(split_high_low(value[:tok, :rank]), axis=1)
    both = dot(token_2, cot_ref[...], 0, 0)
    store_halves(both[:rank] + both[rank:] + error_term_ref[...], mine_ref, other_ref)


def pieces_kernel(mine_ref, got_ref, out_ref):
    for k in range(out_ref.shape[0]):
        columns = pl.ds(k * 128, 128)
        out_ref[k] = (mine_ref[:, columns] + got_ref[:, columns].astype(F32)).astype(BF16)


def sum_kernel(parts_ref, out_ref):
    piece = total_of(parts_ref).astype(BF16)
    for k in range(out_ref.shape[0]):
        out_ref[k] = piece


def inverse_kernel(mine_ref, other_ref, out_ref):
    rank = mine_ref.shape[1]
    low = core_index() == 0
    mine, other = mine_ref[...], other_ref[...]
    gram = jnp.concatenate([jnp.where(low, mine, other), jnp.where(low, other, mine)], axis=0)
    row_of = lax.broadcasted_iota(jnp.int32, (rank, rank), 0)
    column_of = lax.broadcasted_iota(jnp.int32, (rank, rank), 1)
    state = jnp.concatenate([gram, (row_of == column_of).astype(F32)], axis=1)
    rows = [state[8 * b:8 * b + 8] for b in range(rank // 8)]
    index = lax.broadcasted_iota(jnp.int32, (8, 2 * rank), 0)
    for k in range(rank):
        b, r = divmod(k, 8)
        pivot = rows[b][r:r + 1, k:k + 1]
        scale = lax.rsqrt(pivot)
        scale = scale * (1.5 - 0.5 * pivot * scale * scale)
        row = rows[b][r:r + 1] * scale
        for j in range(b, rank // 8):
            factor = rows[j][:, k:k + 1] * scale
            update = rows[j] - factor * row
            if j == b:
                rows[j] = jnp.where(index > r, update, jnp.where(index == r, row, rows[j]))
            else:
                rows[j] = update
    out_ref[...] = jnp.concatenate(rows, axis=0)[:, rank:]


def basis_kernel(replicas, parts_ref, inverse_ref, out_ref):
    value = total_of(parts_ref) * (1.0 / replicas)
    value = dot(inverse_ref[...], value, precision=lax.Precision.HIGHEST).astype(BF16)
    for k in range(out_ref.shape[0]):
        out_ref[k] = value


def ortho_kernel(panel_ref, inverse_ref, out_ref):
    out_ref[...] = dot(panel_ref[...], inverse_ref[...], 0, 1, lax.Precision.HIGHEST).astype(BF16)


def final_kernel(mine_ref, other_ref, ortho_ref, merged_ref, error_ref, basis_ref, basis):
    @pl.when(pl.program_id(0) == 0)
    def _():
        low = core_index() == 0
        pieces = mine_ref.shape[0]
        for k in range(pieces):
            mine, other = mine_ref[k], other_ref[k]
            for place, value in ((k, jnp.where(low, mine, other)), (k + pieces, jnp.where(low, other, mine))):
                columns = pl.ds(place * 128, 128)
                basis[:, columns] = value
                basis_ref[:, columns] = value.astype(F32)

    for c in range(0, error_ref.shape[1], 1024):
        columns = pl.ds(c, 1024)
        approx = dot(ortho_ref[...], basis[:, columns])
        error_ref[:, columns] = (merged_ref[:, columns].astype(F32) - approx).astype(BF16)


def shards(attn, cot, weight, error, warm):
    dp = lax.axis_size("dp")
    group = lax.axis_size("tensor")
    zs = dp // 2
    rank = warm.shape[1]
    tokens, feats = attn.shape
    tok, width = cot.shape
    half = width // 2
    warm = warm.T
    pair = [(i, i ^ 1) for i in range(dp)]
    z_groups = [list(range(0, dp, 2)), list(range(dp - 1, 0, -2))]
    barrier = lax.optimization_barrier

    def swap(value):
        return lax.ppermute(value, "dp", pair)

    def exchange(value, axis, groups=None):
        return lax.all_to_all(value, axis, 0, 0, tiled=True, axis_index_groups=groups)

    cot_all = lax.all_gather(cot, "tensor", axis=0, tiled=True)

    anywhere = pl.BlockSpec(memory_space=pl.ANY)
    q = call(
        token_kernel, shape((group, tok, 2 * rank), BF16), cot, warm,
        ins=[anywhere, anywhere],
        scratch=[pltpu.VMEM((tok, width), BF16), pltpu.VMEM((rank, width), F32), pltpu.SemaphoreType.DMA((4,))],
        flops=4 * tok * width * rank, moved=3 * MB, limit=60,
    )
    q = exchange(q, "tensor").reshape(tokens, 2 * rank)
    e = dot(jnp.concatenate(split_high_low(warm), axis=0), error, 1, 1)
    e = e[:rank] + e[rank:]
    q, e = barrier((q, e))
    half_panel = shape((rank, feats // 2), F32)
    mine, other = call(part_kernel, (half_panel, half_panel), q, attn, e, flops=2 * 128 * feats * tokens, moved=MB)
    spread = call(spread_kernel, shape((zs, rank, feats // 2), BF16), mine, swap(other), moved=MB // 2)
    parts = exchange(spread, "dp", z_groups)
    mine = call(functools.partial(mean_kernel, dp), half_panel, parts, moved=MB // 2)
    other = swap(mine)

    panel, packed = call(
        feature_kernel,
        (shape((rank, feats), F32), shape((group, rank, 2 * rank), BF16)),
        mine, other, attn, flops=4 * tokens * feats * rank, moved=2 * MB,
    )
    parts = exchange(packed, "tensor")
    rows = feats // 2
    error_term = call(
        error_term_kernel, shape((rank, width), F32), panel, error,
        grid=(feats // rows,),
        ins=[pl.BlockSpec((rank, rows), lambda i: (0, i)), pl.BlockSpec((rows, width), lambda i: (i, 0))],
        out_specs=pl.BlockSpec((rank, width), lambda i: (0, 0)),
        flops=4 * feats * width * rank, moved=6 * MB,
    )
    parts, error_term = barrier((parts, error_term))

    half_basis = shape((rank, half), F32)
    mine, other, gram = call(
        basis_term_kernel, (half_basis, shape((rank, half), BF16), shape((rank // 2, rank), F32)), parts, cot, error_term, moved=4 * MB
    )
    packed = call(pieces_kernel, shape((group, rank, half // group), BF16), mine, swap(other), moved=2 * MB)
    parts = exchange(packed, "tensor")
    inverse = call(inverse_kernel, shape((rank, rank), F32), gram, swap(gram), flops=5 * 10**9, moved=MB // 16)
    ortho = call(ortho_kernel, shape((feats, rank), BF16), panel, inverse, flops=10**8, moved=MB // 4)
    parts, inverse, ortho = barrier((parts, inverse, ortho))
    spread = call(sum_kernel, shape((zs, rank, half // group), BF16), parts, moved=MB // 2)
    parts = exchange(spread, "dp", z_groups)
    grad_in = dot(cot_all, weight, 1, 1).astype(BF16)
    parts, grad_in = barrier((parts, grad_in))
    spread = call(
        functools.partial(basis_kernel, dp), shape((group, rank, half // group), BF16), parts, inverse, moved=MB // 2
    )
    mine = exchange(spread, "tensor")
    merged = (dot(attn, cot_all, 0, 0) + error.astype(F32)).astype(BF16)
    mine, merged = barrier((mine, merged))
    other = swap(mine)
    rows = feats // 2
    new_error, new_basis = call(
        final_kernel,
        (shape((feats, width), BF16), shape((rank, width), F32)),
        mine, other, ortho, merged,
        grid=(feats // rows,),
        ins=[pl.BlockSpec(mine.shape, lambda i: (0, 0, 0))] * 2
        + [pl.BlockSpec((rows, rank), lambda i: (i, 0)), pl.BlockSpec((rows, width), lambda i: (i, 0))],
        out_specs=(pl.BlockSpec((rows, width), lambda i: (i, 0)), pl.BlockSpec((rank, width), lambda i: (0, 0))),
        scratch=[pltpu.VMEM((rank, width), BF16)],
        flops=2 * feats * width * rank, moved=10 * MB, limit=60,
    )
    return grad_in, new_error, new_basis.T


def solution(mesh):
    in_specs = (
        P("dp", "tensor"),
        P(("dp", "tensor"), None),
        P("tensor", None),
        P(("dp", "tensor"), None),
        P(),
    )
    out_specs = (P("dp", "tensor"), P(("dp", "tensor"), None), P())
    return jax.shard_map(shards, mesh=mesh, in_specs=in_specs, out_specs=out_specs, check_vma=False)
```

profile of v0, /device:TPU:1, one launch (start us, length us, event | category | flops | bytes accessed | tf_op | source)
XLA Modules:
  0.0 126.4 jit_solution(5899661257186384989)
XLA Ops:
  7.2 0.0 copy-start.4
  7.2 0.0 all-gather.2.cloned.1.call-start
  7.2 0.7 all-gather.2.cloned.1.call-update
  7.9 2.6 %shard_map.76 = bf16[16,48,128]{2,1,0:T(8,128)(2,1)} custom-call(bf16[48,4096]{1,0:T(8,128)(2,1)} %cot_ref.1, f32[64,4096]{1,0:T(8,128)} %bitcast.13), custom_call_target="tpu_custom_call" | custom-call | flops 50331648 | bytes 3145728 | tf_op jit(solution)/shard_map/pallas_call | solution.py:33
  10.6 7.6 %all-to-all-start = ((bf16[16,48,128]{2,1,0:T(8,128)(2,1)}), bf16[16,48,128]{2,1,0:T(8,128)(2,1)S(1)}, u32[]{:S(2)}, u32[]{:S(2)}) async-start(bf16[16,48,128]{2,1,0:T(8,128)(2,1)} %shard_map.76), calls=%async_computation | async-start | bytes 393216 | tf_op jit(solution)/shard_map/all_to_all | solution.py:241
  18.2 1.3 %bitcast_convert_fusion = bf16[64,4096]{1,0:T(8,128)(2,1)S(1)} fusion(f32[4096,64]{0,1:T(8,128)} %param.9), kind=kLoop, calls=%fused_computation.9 | loop fusion | flops 262144 | bytes 1572864 | tf_op jit(solution)/shard_map/convert_element_type | solution.py:21
  19.5 0.0 copy-start.1
  19.5 0.1 subtract_convert_fusion
  19.5 3.8 %fusion = f32[128,512]{1,0:T(8,128)S(1)} fusion(bf16[512,4096]{1,0:T(8,128)(2,1)} %error_ref.1, bf16[64,4096]{1,0:T(8,128)(2,1)S(1)} %subtract_convert_fusion, bf16[64,4096]{1,0:T(8,128)(2,1)S(1)} %bitcast_convert_fusion), kind=kOutput, calls=%fused_computation.2 | convolution fusion | flops 538968064 | bytes 5505024 | tf_op jit(solution)/shard_map/dot_general | solution.py:26
  23.4 1.9 %all-to-all-done = bf16[16,48,128]{2,1,0:T(8,128)(2,1)S(1)} async-done(((bf16[16,48,128]{2,1,0:T(8,128)(2,1)}), bf16[16,48,128]{2,1,0:T(8,128)(2,1)S(1)}, u32[]{:S(2)}, u32[]{:S(2)}) %all-to-all-start) | async-done | bytes 196640 | tf_op jit(solution)/shard_map/all_to_all | solution.py:241
  25.3 0.0 copy-done.1
  25.3 0.3 shard_map.77
  25.6 0.0 copy-start.2
  25.6 2.1 %collective-permute-start = (f32[64,256]{1,0:T(8,128)S(1)}, f32[64,256]{1,0:T(8,128)S(1)}, u32[]{:S(2)}, u32[]{:S(2)}) collective-permute-start(f32[64,256]{1,0:T(8,128)S(1)} %get-tuple-element.26), channel_id=1, source_target_pairs={{0,16},{16,0},{32,48},{48,32},{64,80},{80,64},{96,112},{112,96},{1... | collective-permute-start | bytes 196616 | tf_op jit(solution)/shard_map/ppermute | solution.py:238
  27.7 0.9 collective-permute-done.got_ref
  28.6 13.9 %all_to_all.30.parts_ref = bf16[8,64,256]{2,1,0:T(8,128)(2,1)S(1)} all-to-all(bf16[8,64,256]{2,1,0:T(8,128)(2,1)S(1)} %shard_map.78), channel_id=1, replica_groups={{0,32,64,96,128,160,192,224},{240,208,176,144,112,80,48,16},{1,33,65,97..., dimensions={0} | all-to-all | bytes 524288 | tf_op jit(solution)/shard_map/all_to_all | solution.py:241
  42.6 5.9 %collective-permute-start.1 = (f32[64,256]{1,0:T(8,128)S(1)}, f32[64,256]{1,0:T(8,128)S(1)}, u32[]{:S(2)}, u32[]{:S(2)}) collective-permute-start(f32[64,256]{1,0:T(8,128)S(1)} %shard_map.79.mine_ref), channel_id=1, source_target_pairs={{0,16},{16,0},{32,48},{48,32},{64,80},{80,64},{96,112},{112,96},{1... | collective-permute-start | bytes 196616 | tf_op jit(solution)/shard_map/ppermute | solution.py:238
  48.5 0.9 collective-permute-done.1.other_ref
  49.4 1.2 shard_map.80
  50.6 4.0 %all-to-all-start.2 = ((bf16[16,64,128]{2,1,0:T(8,128)(2,1)}), bf16[16,64,128]{2,1,0:T(8,128)(2,1)S(1)}, u32[]{:S(2)}, u32[]{:S(2)}) async-start(bf16[16,64,128]{2,1,0:T(8,128)(2,1)} %get-tuple-element.27), calls=%async_computation.2 | async-start | bytes 524288 | tf_op jit(solution)/shard_map/all_to_all | solution.py:241
  54.7 0.0 copy-start
  54.7 2.2 %copy-done = bf16[512,4096]{1,0:T(8,128)(2,1)S(1)} copy-done((bf16[512,4096]{1,0:T(8,128)(2,1)S(1)}, bf16[512,4096]{1,0:T(8,128)(2,1)}, u32[]{:S(2)}) %copy-start) | copy-done | bytes 4194328
  56.9 2.0 %shard_map.81.error_term_ref = f32[64,4096]{1,0:T(8,128)S(1)} custom-call(f32[64,512]{1,0:T(8,128)S(1)} %get-tuple-element.28.panel_ref, bf16[512,4096]{1,0:T(8,128)(2,1)S(1)} %copy-done), custom_call_target="tpu_custom_call" | custom-call | flops 536870912 | bytes 6291456 | tf_op jit(solution)/shard_map/pallas_call | solution.py:33
  58.9 6.0 %all-to-all-done.2.parts_ref = bf16[16,64,128]{2,1,0:T(8,128)(2,1)S(1)} async-done(((bf16[16,64,128]{2,1,0:T(8,128)(2,1)}), bf16[16,64,128]{2,1,0:T(8,128)(2,1)S(1)}, u32[]{:S(2)}, u32[]{:S(2)}) %all-to-all-start.2) | async-done | bytes 262176 | tf_op jit(solution)/shard_map/all_to_all | solution.py:241
  64.9 0.0 copy-done.2
  64.9 0.6 shard_map.82
  65.5 1.9 %collective-permute-start.2 = (bf16[64,2048]{1,0:T(8,128)(2,1)S(1)}, bf16[64,2048]{1,0:T(8,128)(2,1)S(1)}, u32[]{:S(2)}, u32[]{:S(2)}) collective-permute-start(bf16[64,2048]{1,0:T(8,128)(2,1)S(1)} %get-tuple-element.32), channel_id=1, source_target_pairs={{0,16},{16,0},{32,48},{48,32},{64,80},{80,64},{96,112},{112,96},{1... | collective-permute-start | bytes 786440 | tf_op jit(solution)/shard_map/ppermute | solution.py:238
  67.4 0.1 collective-permute-start.3
  67.5 1.1 collective-permute-done.2.got_ref
  68.6 0.7 shard_map.83
  69.3 4.2 %all-to-all-start.3 = ((bf16[16,64,128]{2,1,0:T(8,128)(2,1)}), bf16[16,64,128]{2,1,0:T(8,128)(2,1)S(1)}, u32[]{:S(2)}, u32[]{:S(2)}) async-start(bf16[16,64,128]{2,1,0:T(8,128)(2,1)} %shard_map.83), calls=%async_computation.3 | async-start | bytes 524288 | tf_op jit(solution)/shard_map/all_to_all | solution.py:241
  73.5 0.0 collective-permute-done.3.other_ref
  73.6 5.9 %shard_map.84.inverse_ref = f32[64,64]{1,0:T(8,128)S(1)} custom-call(f32[32,64]{1,0:T(8,128)S(1)} %get-tuple-element.33.mine_ref, f32[32,64]{1,0:T(8,128)S(1)} %collective-permute-done.3.other_ref), custom_call_target="tpu_custom_call" | custom-call | flops 5000000000 | bytes 65536 | tf_op jit(solution)/shard_map/pallas_call | solution.py:33
  79.4 0.4 shard_map.85.ortho_ref
  79.9 0.6 copy-done.3
  80.5 3.3 %all-to-all-done.3.parts_ref = bf16[16,64,128]{2,1,0:T(8,128)(2,1)S(1)} async-done(((bf16[16,64,128]{2,1,0:T(8,128)(2,1)}), bf16[16,64,128]{2,1,0:T(8,128)(2,1)S(1)}, u32[]{:S(2)}, u32[]{:S(2)}) %all-to-all-start.3) | async-done | bytes 262176 | tf_op jit(solution)/shard_map/all_to_all | solution.py:241
  83.8 0.7 shard_map.86
  84.5 4.0 %all-to-all-start.4 = ((bf16[8,64,128]{2,1,0:T(8,128)(2,1)}), bf16[8,64,128]{2,1,0:T(8,128)(2,1)S(1)}, u32[]{:S(2)}, u32[]{:S(2)}) async-start(bf16[8,64,128]{2,1,0:T(8,128)(2,1)} %shard_map.86), calls=%async_computation.4 | async-start | bytes 262144 | tf_op jit(solution)/shard_map/all_to_all | solution.py:241
  88.4 8.3 %convolution_convert_fusion = bf16[768,512]{1,0:T(8,128)(2,1)} fusion(bf16[768,4096]{1,0:T(8,128)(2,1)} %all-gather.2.cloned.1.call-done, bf16[512,4096]{1,0:T(8,128)(2,1)} %param.7), kind=kOutput, calls=%fused_computation.1 | convolution fusion | flops 3221618688 | bytes 11272192 | tf_op jit(solution)/shard_map/dot_general | solution.py:26
  96.8 0.0 all-to-all-done.4.parts_ref
  96.8 0.9 shard_map.87
  97.7 4.6 %all-to-all-start.5 = ((bf16[16,64,128]{2,1,0:T(8,128)(2,1)}), bf16[16,64,128]{2,1,0:T(8,128)(2,1)S(1)}, u32[]{:S(2)}, u32[]{:S(2)}) async-start(bf16[16,64,128]{2,1,0:T(8,128)(2,1)} %shard_map.87), calls=%async_computation.5 | async-start | bytes 524288 | tf_op jit(solution)/shard_map/all_to_all | solution.py:241
  102.3 8.6 %add_convert_fusion.merged_ref = bf16[512,4096]{1,0:T(8,128)(2,1)} fusion(bf16[512,4096]{1,0:T(8,128)(2,1)} %error_ref.1, bf16[768,512]{1,0:T(8,128)(2,1)S(1)} %copy-done.1, bf16[768,4096]{1,0:T(8,128)(2,1)} %all-gather.2.cloned.1.call-done), kind=kOutput, calls=%fused_computation | convolution fusion | flops 3227516928 | bytes 15466496 | tf_op jit(solution)/shard_map/dot_general | solution.py:26
  110.8 0.0 all-to-all-done.5.mine_ref
  110.8 1.9 %collective-permute-start.4 = (bf16[16,64,128]{2,1,0:T(8,128)(2,1)S(1)}, bf16[16,64,128]{2,1,0:T(8,128)(2,1)S(1)}, u32[]{:S(2)}, u32[]{:S(2)}) collective-permute-start(bf16[16,64,128]{2,1,0:T(8,128)(2,1)S(1)} %all-to-all-done.5.mine_ref), channel_id=1, source_target_pairs={{0,16},{16,0},{32,48},{48,32},{64,80},{80,64},{96,112},{112,96},{1... | collective-permute-start | bytes 786440 | tf_op jit(solution)/shard_map/ppermute | solution.py:238
  112.7 1.2 collective-permute-done.4.other_ref
  113.9 0.7 copy-done.6
  114.6 4.9 %shard_map.88 = (bf16[512,4096]{1,0:T(8,128)(2,1)}, f32[64,4096]{1,0:T(8,128)}) custom-call(bf16[16,64,128]{2,1,0:T(8,128)(2,1)} %copy-done.5, bf16[16,64,128]{2,1,0:T(8,128)(2,1)} %copy-done.6, bf16[512,64]{1,0:T(8,128)(2,1)} %copy-done.3, bf16[512,4096]{1,0:T(8,128)(2,1)} %add_convert_fusion.merged_ref), custom_call_target="tpu_custom_call" | custom-call | flops 268435456 | bytes 10485760 | tf_op jit(solution)/shard_map/pallas_call | solution.py:33
  (9 shorter events, 0.1 us)
Async XLA Ops:
  7.2 12.3 %copy-start.4 = (f32[4096,64]{0,1:T(8,128)S(1)}, f32[4096,64]{0,1:T(8,128)}, u32[]{:S(2)}) copy-start(f32[4096,64]{0,1:T(8,128)} %param.9) | copy-start | bytes 3145732
  7.2 81.3 %all-gather.2.cloned.1.call-start = ((), (), s32[]{:S(2)}) async-start(), calls=%async_computation.6 | async-start | bytes 6684672 | tf_op jit(solution)/shard_map/all_gather | solution.py:243
  10.6 14.8 %all-to-all-start = ((bf16[16,48,128]{2,1,0:T(8,128)(2,1)}), bf16[16,48,128]{2,1,0:T(8,128)(2,1)S(1)}, u32[]{:S(2)}, u32[]{:S(2)}) async-start(bf16[16,48,128]{2,1,0:T(8,128)(2,1)} %shard_map.76), calls=%async_computation | async-start | bytes 393216 | tf_op jit(solution)/shard_map/all_to_all | solution.py:241
  19.5 5.9 %copy-start.1 = (bf16[768,512]{1,0:T(8,128)(2,1)S(1)}, bf16[768,512]{1,0:T(8,128)(2,1)}, u32[]{:S(2)}) copy-start(bf16[768,512]{1,0:T(8,128)(2,1)} %attn_ref.3) | copy-start | bytes 2359300
  25.6 39.3 %copy-start.2 = (bf16[48,4096]{1,0:T(8,128)(2,1)S(1)}, bf16[48,4096]{1,0:T(8,128)(2,1)}, u32[]{:S(2)}) copy-start(bf16[48,4096]{1,0:T(8,128)(2,1)} %cot_ref.1) | copy-start | bytes 1179652
  25.6 3.0 %collective-permute-start = (f32[64,256]{1,0:T(8,128)S(1)}, f32[64,256]{1,0:T(8,128)S(1)}, u32[]{:S(2)}, u32[]{:S(2)}) collective-permute-start(f32[64,256]{1,0:T(8,128)S(1)} %get-tuple-element.26), channel_id=1, source_target_pairs={{0,16},{16,0},{32,48},{48,32},{64,80},{80,64},{96,112},{112,96},{1... | collective-permute-start | bytes 196616 | tf_op jit(solution)/shard_map/ppermute | solution.py:238
  42.6 6.8 %collective-permute-start.1 = (f32[64,256]{1,0:T(8,128)S(1)}, f32[64,256]{1,0:T(8,128)S(1)}, u32[]{:S(2)}, u32[]{:S(2)}) collective-permute-start(f32[64,256]{1,0:T(8,128)S(1)} %shard_map.79.mine_ref), channel_id=1, source_target_pairs={{0,16},{16,0},{32,48},{48,32},{64,80},{80,64},{96,112},{112,96},{1... | collective-permute-start | bytes 196616 | tf_op jit(solution)/shard_map/ppermute | solution.py:238
  50.6 14.3 %all-to-all-start.2 = ((bf16[16,64,128]{2,1,0:T(8,128)(2,1)}), bf16[16,64,128]{2,1,0:T(8,128)(2,1)S(1)}, u32[]{:S(2)}, u32[]{:S(2)}) async-start(bf16[16,64,128]{2,1,0:T(8,128)(2,1)} %get-tuple-element.27), calls=%async_computation.2 | async-start | bytes 524288 | tf_op jit(solution)/shard_map/all_to_all | solution.py:241
  54.7 2.2 %copy-start = (bf16[512,4096]{1,0:T(8,128)(2,1)S(1)}, bf16[512,4096]{1,0:T(8,128)(2,1)}, u32[]{:S(2)}) copy-start(bf16[512,4096]{1,0:T(8,128)(2,1)} %error_ref.1) | copy-start | bytes 12582916
  65.5 3.1 %collective-permute-start.2 = (bf16[64,2048]{1,0:T(8,128)(2,1)S(1)}, bf16[64,2048]{1,0:T(8,128)(2,1)S(1)}, u32[]{:S(2)}, u32[]{:S(2)}) collective-permute-start(bf16[64,2048]{1,0:T(8,128)(2,1)S(1)} %get-tuple-element.32), channel_id=1, source_target_pairs={{0,16},{16,0},{32,48},{48,32},{64,80},{80,64},{96,112},{112,96},{1... | collective-permute-start | bytes 786440 | tf_op jit(solution)/shard_map/ppermute | solution.py:238
  67.4 6.1 %collective-permute-start.3 = (f32[32,64]{1,0:T(8,128)S(1)}, f32[32,64]{1,0:T(8,128)S(1)}, u32[]{:S(2)}, u32[]{:S(2)}) collective-permute-start(f32[32,64]{1,0:T(8,128)S(1)} %get-tuple-element.33.mine_ref), channel_id=1, source_target_pairs={{0,16},{16,0},{32,48},{48,32},{64,80},{80,64},{96,112},{112,96},{1... | collective-permute-start | bytes 24584 | tf_op jit(solution)/shard_map/ppermute | solution.py:238
  69.3 14.5 %all-to-all-start.3 = ((bf16[16,64,128]{2,1,0:T(8,128)(2,1)}), bf16[16,64,128]{2,1,0:T(8,128)(2,1)S(1)}, u32[]{:S(2)}, u32[]{:S(2)}) async-start(bf16[16,64,128]{2,1,0:T(8,128)(2,1)} %shard_map.83), calls=%async_computation.3 | async-start | bytes 524288 | tf_op jit(solution)/shard_map/all_to_all | solution.py:241
  79.9 0.6 copy-start.3
  84.5 12.3 %all-to-all-start.4 = ((bf16[8,64,128]{2,1,0:T(8,128)(2,1)}), bf16[8,64,128]{2,1,0:T(8,128)(2,1)S(1)}, u32[]{:S(2)}, u32[]{:S(2)}) async-start(bf16[8,64,128]{2,1,0:T(8,128)(2,1)} %shard_map.86), calls=%async_computation.4 | async-start | bytes 262144 | tf_op jit(solution)/shard_map/all_to_all | solution.py:241
  97.7 13.2 %all-to-all-start.5 = ((bf16[16,64,128]{2,1,0:T(8,128)(2,1)}), bf16[16,64,128]{2,1,0:T(8,128)(2,1)S(1)}, u32[]{:S(2)}, u32[]{:S(2)}) async-start(bf16[16,64,128]{2,1,0:T(8,128)(2,1)} %shard_map.87), calls=%async_computation.5 | async-start | bytes 524288 | tf_op jit(solution)/shard_map/all_to_all | solution.py:241
  110.8 3.0 %copy-start.5 = (bf16[16,64,128]{2,1,0:T(8,128)(2,1)}, bf16[16,64,128]{2,1,0:T(8,128)(2,1)S(1)}, u32[]{:S(2)}) copy-start(bf16[16,64,128]{2,1,0:T(8,128)(2,1)S(1)} %all-to-all-done.5.mine_ref) | copy-start | bytes 786436
  110.8 3.0 %collective-permute-start.4 = (bf16[16,64,128]{2,1,0:T(8,128)(2,1)S(1)}, bf16[16,64,128]{2,1,0:T(8,128)(2,1)S(1)}, u32[]{:S(2)}, u32[]{:S(2)}) collective-permute-start(bf16[16,64,128]{2,1,0:T(8,128)(2,1)S(1)} %all-to-all-done.5.mine_ref), channel_id=1, source_target_pairs={{0,16},{16,0},{32,48},{48,32},{64,80},{80,64},{96,112},{112,96},{1... | collective-permute-start | bytes 786440 | tf_op jit(solution)/shard_map/ppermute | solution.py:238
  113.9 0.7 copy-start.6
Sparse Core Ops, SparseCore 0:
  10.5 75.7 all-gather.1
where the time goes:
time: 127 us; the launch traced here: 126 us
  starting transfers between devices  36.3 us (29%)
  matrix products  20.7 us (16%)
  Pallas kernels  20.4 us (16%)
  waiting for transfers between devices  15.9 us (13%)
  between operations  14.2 us (11%)
  blocking collectives  13.9 us (11%)
  local copies, waits for them, and re-layouts  3.53 us (3%)
  other arithmetic  1.36 us (1%)
    all_to_all x5, starting transfers between devices, exchange(): lax.all_to_all(value, axis, 0, 0, tiled=True, axis_index_groups=groups)  24.4 us
    dot_general x3, matrix products, dot(): lax.dot_general(a, b, (((ca,), (cb,)), ((), ())), preferred_element_type=...  20.7 us
    pallas_call x13, Pallas kernels, call(): pl.pallas_call(kernel, out_shape=outs, in_specs=ins or [VMEM] * len(args)...  20.4 us
    all_to_all x1, blocking collectives, exchange(): lax.all_to_all(value, axis, 0, 0, tiled=True, axis_index_groups=groups)  13.9 us
    ppermute x5, starting transfers between devices, swap(): return lax.ppermute(value, 'dp', pair)  11.9 us
    all_to_all x5, waiting for transfers between devices, exchange(): lax.all_to_all(value, axis, 0, 0, tiled=True, axis_index_groups=groups)  11.2 us
    ppermute x5, waiting for transfers between devices, swap(): return lax.ppermute(value, 'dp', pair)  4.03 us
    unnamed x14, local copies, waits for them, and re-layouts  3.53 us
  transfers between devices with their start and end apart: 11, of which 7 were waited for; matrix products, arithmetic and copies ran while one was open for 17% of the time, Pallas kernels for 11%

commit v1 on v0

--- a/solution.py
+++ b/solution.py
@@ -231,7 +231,8 @@
     half = width // 2
     warm = warm.T
     pair = [(i, i ^ 1) for i in range(dp)]
-    z_groups = [list(range(0, dp, 2)), list(range(dp - 1, 0, -2))]
+    z_up = [list(range(c, dp, 2)) for c in range(2)]
+    z_down = [planes[::-1] for planes in z_up]
     barrier = lax.optimization_barrier
 
     def swap(value):
@@ -256,7 +257,7 @@
     half_panel = shape((rank, feats // 2), F32)
     mine, other = call(part_kernel, (half_panel, half_panel), q, attn, e, flops=2 * 128 * feats * tokens, moved=MB)
     spread = call(spread_kernel, shape((zs, rank, feats // 2), BF16), mine, swap(other), moved=MB // 2)
-    parts = exchange(spread, "dp", z_groups)
+    parts = exchange(spread, "dp", z_down)
     mine = call(functools.partial(mean_kernel, dp), half_panel, parts, moved=MB // 2)
     other = swap(mine)
 
@@ -286,7 +287,7 @@
     ortho = call(ortho_kernel, shape((feats, rank), BF16), panel, inverse, flops=10**8, moved=MB // 4)
     parts, inverse, ortho = barrier((parts, inverse, ortho))
     spread = call(sum_kernel, shape((zs, rank, half // group), BF16), parts, moved=MB // 2)
-    parts = exchange(spread, "dp", z_groups)
+    parts = exchange(spread, "dp", z_up)
     grad_in = dot(cot_all, weight, 1, 1).astype(BF16)
     parts, grad_in = barrier((parts, grad_in))
     spread = call(

time: 127 us -> 127 us (level)
    ppermute x5, starting transfers between devices: 11.9 us -> 9.21 us  [swap(): return lax.ppermute(value, 'dp', pair)]
    all_to_all x5, starting transfers between devices: 24.4 us -> 26.6 us  [exchange(): lax.all_to_all(value, axis, 0, 0, tiled=True, axis_index_groups=groups)]
  transfers between devices with their start and end apart: 11 -> 11, of which waited for: 7 -> 7; matrix products, arithmetic and copies ran while one was open for 17% -> 18% of each run, Pallas kernels for 11% -> 12%
where the time goes in v1:
time: 127 us; the launch traced here: 126 us
  starting transfers between devices  35.9 us (28%)
  matrix products  20.7 us (16%)
  Pallas kernels  20.4 us (16%)
  waiting for transfers between devices  15.3 us (12%)
  between operations  14.2 us (11%)
  blocking collectives  14.1 us (11%)
  local copies, waits for them, and re-layouts  4.01 us (3%)
  other arithmetic  1.36 us (1%)
    all_to_all x5, starting transfers between devices, exchange(): lax.all_to_all(value, axis, 0, 0, tiled=True, axis_index_groups=groups)  26.6 us
    dot_general x3, matrix products, dot(): lax.dot_general(a, b, (((ca,), (cb,)), ((), ())), preferred_element_type=...  20.7 us
    pallas_call x13, Pallas kernels, call(): pl.pallas_call(kernel, out_shape=outs, in_specs=ins or [VMEM] * len(args)...  20.4 us
    all_to_all x1, blocking collectives, exchange(): lax.all_to_all(value, axis, 0, 0, tiled=True, axis_index_groups=groups)  14.1 us
    all_to_all x5, waiting for transfers between devices, exchange(): lax.all_to_all(value, axis, 0, 0, tiled=True, axis_index_groups=groups)  10.6 us
    ppermute x5, starting transfers between devices, swap(): return lax.ppermute(value, 'dp', pair)  9.21 us
    ppermute x5, waiting for transfers between devices, swap(): return lax.ppermute(value, 'dp', pair)  4.03 us
    unnamed x14, local copies, waits for them, and re-layouts  4.01 us
  transfers between devices with their start and end apart: 11, of which 7 were waited for; matrix products, arithmetic and copies ran while one was open for 18% of the time, Pallas kernels for 12%

profile of v1, /device:TPU:1, one launch (start us, length us, event | category | flops | bytes accessed | tf_op | source)
XLA Modules:
  0.0 125.9 jit_solution(1771093976086700926)
XLA Ops:
  7.2 0.0 copy-start.4
  7.2 0.0 all-gather.2.cloned.1.call-start
  7.2 0.7 all-gather.2.cloned.1.call-update
  7.9 2.6 %shard_map.76 = bf16[16,48,128]{2,1,0:T(8,128)(2,1)} custom-call(bf16[48,4096]{1,0:T(8,128)(2,1)} %cot_ref.1, f32[64,4096]{1,0:T(8,128)} %bitcast.13), custom_call_target="tpu_custom_call" | custom-call | flops 50331648 | bytes 3145728 | tf_op jit(solution)/shard_map/pallas_call | solution.py:33
  10.6 7.6 %all-to-all-start = ((bf16[16,48,128]{2,1,0:T(8,128)(2,1)}), bf16[16,48,128]{2,1,0:T(8,128)(2,1)S(1)}, u32[]{:S(2)}, u32[]{:S(2)}) async-start(bf16[16,48,128]{2,1,0:T(8,128)(2,1)} %shard_map.76), calls=%async_computation | async-start | bytes 393216 | tf_op jit(solution)/shard_map/all_to_all | solution.py:242
  18.2 1.3 %bitcast_convert_fusion = bf16[64,4096]{1,0:T(8,128)(2,1)S(1)} fusion(f32[4096,64]{0,1:T(8,128)} %param.9), kind=kLoop, calls=%fused_computation.9 | loop fusion | flops 262144 | bytes 1572864 | tf_op jit(solution)/shard_map/convert_element_type | solution.py:21
  19.5 0.0 copy-start.1
  19.5 0.1 subtract_convert_fusion
  19.5 3.8 %fusion = f32[128,512]{1,0:T(8,128)S(1)} fusion(bf16[512,4096]{1,0:T(8,128)(2,1)} %error_ref.1, bf16[64,4096]{1,0:T(8,128)(2,1)S(1)} %subtract_convert_fusion, bf16[64,4096]{1,0:T(8,128)(2,1)S(1)} %bitcast_convert_fusion), kind=kOutput, calls=%fused_computation.2 | convolution fusion | flops 538968064 | bytes 5505024 | tf_op jit(solution)/shard_map/dot_general | solution.py:26
  23.4 1.9 %all-to-all-done = bf16[16,48,128]{2,1,0:T(8,128)(2,1)S(1)} async-done(((bf16[16,48,128]{2,1,0:T(8,128)(2,1)}), bf16[16,48,128]{2,1,0:T(8,128)(2,1)S(1)}, u32[]{:S(2)}, u32[]{:S(2)}) %all-to-all-start) | async-done | bytes 196640 | tf_op jit(solution)/shard_map/all_to_all | solution.py:242
  25.3 0.0 copy-done.1
  25.3 0.3 shard_map.77
  25.6 0.0 copy-start.2
  25.6 2.1 %collective-permute-start = (f32[64,256]{1,0:T(8,128)S(1)}, f32[64,256]{1,0:T(8,128)S(1)}, u32[]{:S(2)}, u32[]{:S(2)}) collective-permute-start(f32[64,256]{1,0:T(8,128)S(1)} %get-tuple-element.26), channel_id=1, source_target_pairs={{0,16},{16,0},{32,48},{48,32},{64,80},{80,64},{96,112},{112,96},{1... | collective-permute-start | bytes 196616 | tf_op jit(solution)/shard_map/ppermute | solution.py:239
  27.7 0.9 collective-permute-done.got_ref
  28.6 14.1 %all_to_all.30.parts_ref = bf16[8,64,256]{2,1,0:T(8,128)(2,1)S(1)} all-to-all(bf16[8,64,256]{2,1,0:T(8,128)(2,1)S(1)} %shard_map.78), channel_id=1, replica_groups={{224,192,160,128,96,64,32,0},{240,208,176,144,112,80,48,16},{225,193,16..., dimensions={0} | all-to-all | bytes 524288 | tf_op jit(solution)/shard_map/all_to_all | solution.py:242
  42.8 2.5 %collective-permute-start.1 = (f32[64,256]{1,0:T(8,128)S(1)}, f32[64,256]{1,0:T(8,128)S(1)}, u32[]{:S(2)}, u32[]{:S(2)}) collective-permute-start(f32[64,256]{1,0:T(8,128)S(1)} %shard_map.79.mine_ref), channel_id=1, source_target_pairs={{0,16},{16,0},{32,48},{48,32},{64,80},{80,64},{96,112},{112,96},{1... | collective-permute-start | bytes 196616 | tf_op jit(solution)/shard_map/ppermute | solution.py:239
  45.2 0.9 collective-permute-done.1.other_ref
  46.1 1.2 shard_map.80
  47.3 4.0 %all-to-all-start.2 = ((bf16[16,64,128]{2,1,0:T(8,128)(2,1)}), bf16[16,64,128]{2,1,0:T(8,128)(2,1)S(1)}, u32[]{:S(2)}, u32[]{:S(2)}) async-start(bf16[16,64,128]{2,1,0:T(8,128)(2,1)} %get-tuple-element.27), calls=%async_computation.2 | async-start | bytes 524288 | tf_op jit(solution)/shard_map/all_to_all | solution.py:242
  51.4 0.0 copy-start
  51.4 2.7 %copy-done = bf16[512,4096]{1,0:T(8,128)(2,1)S(1)} copy-done((bf16[512,4096]{1,0:T(8,128)(2,1)S(1)}, bf16[512,4096]{1,0:T(8,128)(2,1)}, u32[]{:S(2)}) %copy-start) | copy-done | bytes 4194328
  54.1 2.0 %shard_map.81.error_term_ref = f32[64,4096]{1,0:T(8,128)S(1)} custom-call(f32[64,512]{1,0:T(8,128)S(1)} %get-tuple-element.28.panel_ref, bf16[512,4096]{1,0:T(8,128)(2,1)S(1)} %copy-done), custom_call_target="tpu_custom_call" | custom-call | flops 536870912 | bytes 6291456 | tf_op jit(solution)/shard_map/pallas_call | solution.py:33
  56.1 5.4 %all-to-all-done.2.parts_ref = bf16[16,64,128]{2,1,0:T(8,128)(2,1)S(1)} async-done(((bf16[16,64,128]{2,1,0:T(8,128)(2,1)}), bf16[16,64,128]{2,1,0:T(8,128)(2,1)S(1)}, u32[]{:S(2)}, u32[]{:S(2)}) %all-to-all-start.2) | async-done | bytes 262176 | tf_op jit(solution)/shard_map/all_to_all | solution.py:242
  61.5 0.6 shard_map.82
  62.0 1.8 %collective-permute-start.2 = (bf16[64,2048]{1,0:T(8,128)(2,1)S(1)}, bf16[64,2048]{1,0:T(8,128)(2,1)S(1)}, u32[]{:S(2)}, u32[]{:S(2)}) collective-permute-start(bf16[64,2048]{1,0:T(8,128)(2,1)S(1)} %get-tuple-element.32), channel_id=1, source_target_pairs={{0,16},{16,0},{32,48},{48,32},{64,80},{80,64},{96,112},{112,96},{1... | collective-permute-start | bytes 786440 | tf_op jit(solution)/shard_map/ppermute | solution.py:239
  63.8 0.1 collective-permute-start.3
  63.9 1.1 collective-permute-done.2.got_ref
  65.0 0.7 shard_map.83
  65.7 4.2 %all-to-all-start.3 = ((bf16[16,64,128]{2,1,0:T(8,128)(2,1)}), bf16[16,64,128]{2,1,0:T(8,128)(2,1)S(1)}, u32[]{:S(2)}, u32[]{:S(2)}) async-start(bf16[16,64,128]{2,1,0:T(8,128)(2,1)} %shard_map.83), calls=%async_computation.3 | async-start | bytes 524288 | tf_op jit(solution)/shard_map/all_to_all | solution.py:242
  70.0 0.0 collective-permute-done.3.other_ref
  70.0 5.9 %shard_map.84.inverse_ref = f32[64,64]{1,0:T(8,128)S(1)} custom-call(f32[32,64]{1,0:T(8,128)S(1)} %get-tuple-element.33.mine_ref, f32[32,64]{1,0:T(8,128)S(1)} %collective-permute-done.3.other_ref), custom_call_target="tpu_custom_call" | custom-call | flops 5000000000 | bytes 65536 | tf_op jit(solution)/shard_map/pallas_call | solution.py:33
  75.9 0.4 shard_map.85.ortho_ref
  76.3 0.6 copy-done.3
  77.0 3.3 %all-to-all-done.3.parts_ref = bf16[16,64,128]{2,1,0:T(8,128)(2,1)S(1)} async-done(((bf16[16,64,128]{2,1,0:T(8,128)(2,1)}), bf16[16,64,128]{2,1,0:T(8,128)(2,1)S(1)}, u32[]{:S(2)}, u32[]{:S(2)}) %all-to-all-start.3) | async-done | bytes 262176 | tf_op jit(solution)/shard_map/all_to_all | solution.py:242
  80.2 0.7 shard_map.86
  80.9 6.1 %all-to-all-start.4 = ((bf16[8,64,128]{2,1,0:T(8,128)(2,1)}), bf16[8,64,128]{2,1,0:T(8,128)(2,1)S(1)}, u32[]{:S(2)}, u32[]{:S(2)}) async-start(bf16[8,64,128]{2,1,0:T(8,128)(2,1)} %shard_map.86), calls=%async_computation.4 | async-start | bytes 262144 | tf_op jit(solution)/shard_map/all_to_all | solution.py:242
  87.1 0.0 all-gather.2.cloned.1.call-done
  87.1 8.3 %convolution_convert_fusion = bf16[768,512]{1,0:T(8,128)(2,1)} fusion(bf16[768,4096]{1,0:T(8,128)(2,1)} %all-gather.2.cloned.1.call-done, bf16[512,4096]{1,0:T(8,128)(2,1)} %param.7), kind=kOutput, calls=%fused_computation.1 | convolution fusion | flops 3221618688 | bytes 11272192 | tf_op jit(solution)/shard_map/dot_general | solution.py:26
  95.4 0.0 all-to-all-done.4.parts_ref
  95.4 0.9 shard_map.87
  96.3 4.6 %all-to-all-start.5 = ((bf16[16,64,128]{2,1,0:T(8,128)(2,1)}), bf16[16,64,128]{2,1,0:T(8,128)(2,1)S(1)}, u32[]{:S(2)}, u32[]{:S(2)}) async-start(bf16[16,64,128]{2,1,0:T(8,128)(2,1)} %shard_map.87), calls=%async_computation.5 | async-start | bytes 524288 | tf_op jit(solution)/shard_map/all_to_all | solution.py:242
  100.9 8.6 %add_convert_fusion.merged_ref = bf16[512,4096]{1,0:T(8,128)(2,1)} fusion(bf16[512,4096]{1,0:T(8,128)(2,1)} %error_ref.1, bf16[768,512]{1,0:T(8,128)(2,1)S(1)} %copy-done.1, bf16[768,4096]{1,0:T(8,128)(2,1)} %all-gather.2.cloned.1.call-done), kind=kOutput, calls=%fused_computation | convolution fusion | flops 3227516928 | bytes 15466496 | tf_op jit(solution)/shard_map/dot_general | solution.py:26
  109.5 0.0 all-to-all-done.5.mine_ref
  109.5 2.8 %collective-permute-start.4 = (bf16[16,64,128]{2,1,0:T(8,128)(2,1)S(1)}, bf16[16,64,128]{2,1,0:T(8,128)(2,1)S(1)}, u32[]{:S(2)}, u32[]{:S(2)}) collective-permute-start(bf16[16,64,128]{2,1,0:T(8,128)(2,1)S(1)} %all-to-all-done.5.mine_ref), channel_id=1, source_target_pairs={{0,16},{16,0},{32,48},{48,32},{64,80},{80,64},{96,112},{112,96},{1... | collective-permute-start | bytes 786440 | tf_op jit(solution)/shard_map/ppermute | solution.py:239
  112.3 1.2 collective-permute-done.4.other_ref
  113.5 0.7 copy-done.6
  114.1 4.9 %shard_map.88 = (bf16[512,4096]{1,0:T(8,128)(2,1)}, f32[64,4096]{1,0:T(8,128)}) custom-call(bf16[16,64,128]{2,1,0:T(8,128)(2,1)} %copy-done.5, bf16[16,64,128]{2,1,0:T(8,128)(2,1)} %copy-done.6, bf16[512,64]{1,0:T(8,128)(2,1)} %copy-done.3, bf16[512,4096]{1,0:T(8,128)(2,1)} %add_convert_fusion.merged_ref), custom_call_target="tpu_custom_call" | custom-call | flops 268435456 | bytes 10485760 | tf_op jit(solution)/shard_map/pallas_call | solution.py:33
  (9 shorter events, 0.1 us)
Async XLA Ops:
  7.2 12.3 %copy-start.4 = (f32[4096,64]{0,1:T(8,128)S(1)}, f32[4096,64]{0,1:T(8,128)}, u32[]{:S(2)}) copy-start(f32[4096,64]{0,1:T(8,128)} %param.9) | copy-start | bytes 3145732
  7.2 79.9 %all-gather.2.cloned.1.call-start = ((), (), s32[]{:S(2)}) async-start(), calls=%async_computation.6 | async-start | bytes 6684672 | tf_op jit(solution)/shard_map/all_gather | solution.py:244
  10.6 14.8 %all-to-all-start = ((bf16[16,48,128]{2,1,0:T(8,128)(2,1)}), bf16[16,48,128]{2,1,0:T(8,128)(2,1)S(1)}, u32[]{:S(2)}, u32[]{:S(2)}) async-start(bf16[16,48,128]{2,1,0:T(8,128)(2,1)} %shard_map.76), calls=%async_computation | async-start | bytes 393216 | tf_op jit(solution)/shard_map/all_to_all | solution.py:242
  19.5 5.9 %copy-start.1 = (bf16[768,512]{1,0:T(8,128)(2,1)S(1)}, bf16[768,512]{1,0:T(8,128)(2,1)}, u32[]{:S(2)}) copy-start(bf16[768,512]{1,0:T(8,128)(2,1)} %attn_ref.3) | copy-start | bytes 2359300
  25.6 35.8 %copy-start.2 = (bf16[48,4096]{1,0:T(8,128)(2,1)S(1)}, bf16[48,4096]{1,0:T(8,128)(2,1)}, u32[]{:S(2)}) copy-start(bf16[48,4096]{1,0:T(8,128)(2,1)} %cot_ref.1) | copy-start | bytes 1179652
  25.6 3.0 %collective-permute-start = (f32[64,256]{1,0:T(8,128)S(1)}, f32[64,256]{1,0:T(8,128)S(1)}, u32[]{:S(2)}, u32[]{:S(2)}) collective-permute-start(f32[64,256]{1,0:T(8,128)S(1)} %get-tuple-element.26), channel_id=1, source_target_pairs={{0,16},{16,0},{32,48},{48,32},{64,80},{80,64},{96,112},{112,96},{1... | collective-permute-start | bytes 196616 | tf_op jit(solution)/shard_map/ppermute | solution.py:239
  42.8 3.4 %collective-permute-start.1 = (f32[64,256]{1,0:T(8,128)S(1)}, f32[64,256]{1,0:T(8,128)S(1)}, u32[]{:S(2)}, u32[]{:S(2)}) collective-permute-start(f32[64,256]{1,0:T(8,128)S(1)} %shard_map.79.mine_ref), channel_id=1, source_target_pairs={{0,16},{16,0},{32,48},{48,32},{64,80},{80,64},{96,112},{112,96},{1... | collective-permute-start | bytes 196616 | tf_op jit(solution)/shard_map/ppermute | solution.py:239
  47.3 14.1 %all-to-all-start.2 = ((bf16[16,64,128]{2,1,0:T(8,128)(2,1)}), bf16[16,64,128]{2,1,0:T(8,128)(2,1)S(1)}, u32[]{:S(2)}, u32[]{:S(2)}) async-start(bf16[16,64,128]{2,1,0:T(8,128)(2,1)} %get-tuple-element.27), calls=%async_computation.2 | async-start | bytes 524288 | tf_op jit(solution)/shard_map/all_to_all | solution.py:242
  51.4 2.7 %copy-start = (bf16[512,4096]{1,0:T(8,128)(2,1)S(1)}, bf16[512,4096]{1,0:T(8,128)(2,1)}, u32[]{:S(2)}) copy-start(bf16[512,4096]{1,0:T(8,128)(2,1)} %error_ref.1) | copy-start | bytes 12582916
  62.0 3.0 %collective-permute-start.2 = (bf16[64,2048]{1,0:T(8,128)(2,1)S(1)}, bf16[64,2048]{1,0:T(8,128)(2,1)S(1)}, u32[]{:S(2)}, u32[]{:S(2)}) collective-permute-start(bf16[64,2048]{1,0:T(8,128)(2,1)S(1)} %get-tuple-element.32), channel_id=1, source_target_pairs={{0,16},{16,0},{32,48},{48,32},{64,80},{80,64},{96,112},{112,96},{1... | collective-permute-start | bytes 786440 | tf_op jit(solution)/shard_map/ppermute | solution.py:239
  63.8 6.2 %collective-permute-start.3 = (f32[32,64]{1,0:T(8,128)S(1)}, f32[32,64]{1,0:T(8,128)S(1)}, u32[]{:S(2)}, u32[]{:S(2)}) collective-permute-start(f32[32,64]{1,0:T(8,128)S(1)} %get-tuple-element.33.mine_ref), channel_id=1, source_target_pairs={{0,16},{16,0},{32,48},{48,32},{64,80},{80,64},{96,112},{112,96},{1... | collective-permute-start | bytes 24584 | tf_op jit(solution)/shard_map/ppermute | solution.py:239
  65.7 14.5 %all-to-all-start.3 = ((bf16[16,64,128]{2,1,0:T(8,128)(2,1)}), bf16[16,64,128]{2,1,0:T(8,128)(2,1)S(1)}, u32[]{:S(2)}, u32[]{:S(2)}) async-start(bf16[16,64,128]{2,1,0:T(8,128)(2,1)} %shard_map.83), calls=%async_computation.3 | async-start | bytes 524288 | tf_op jit(solution)/shard_map/all_to_all | solution.py:242
  76.3 0.6 copy-start.3
  80.9 14.5 %all-to-all-start.4 = ((bf16[8,64,128]{2,1,0:T(8,128)(2,1)}), bf16[8,64,128]{2,1,0:T(8,128)(2,1)S(1)}, u32[]{:S(2)}, u32[]{:S(2)}) async-start(bf16[8,64,128]{2,1,0:T(8,128)(2,1)} %shard_map.86), calls=%async_computation.4 | async-start | bytes 262144 | tf_op jit(solution)/shard_map/all_to_all | solution.py:242
  96.3 13.2 %all-to-all-start.5 = ((bf16[16,64,128]{2,1,0:T(8,128)(2,1)}), bf16[16,64,128]{2,1,0:T(8,128)(2,1)S(1)}, u32[]{:S(2)}, u32[]{:S(2)}) async-start(bf16[16,64,128]{2,1,0:T(8,128)(2,1)} %shard_map.87), calls=%async_computation.5 | async-start | bytes 524288 | tf_op jit(solution)/shard_map/all_to_all | solution.py:242
  109.5 4.0 %copy-start.5 = (bf16[16,64,128]{2,1,0:T(8,128)(2,1)}, bf16[16,64,128]{2,1,0:T(8,128)(2,1)S(1)}, u32[]{:S(2)}) copy-start(bf16[16,64,128]{2,1,0:T(8,128)(2,1)S(1)} %all-to-all-done.5.mine_ref) | copy-start | bytes 786436
  109.5 4.0 %collective-permute-start.4 = (bf16[16,64,128]{2,1,0:T(8,128)(2,1)S(1)}, bf16[16,64,128]{2,1,0:T(8,128)(2,1)S(1)}, u32[]{:S(2)}, u32[]{:S(2)}) collective-permute-start(bf16[16,64,128]{2,1,0:T(8,128)(2,1)S(1)} %all-to-all-done.5.mine_ref), channel_id=1, source_target_pairs={{0,16},{16,0},{32,48},{48,32},{64,80},{80,64},{96,112},{112,96},{1... | collective-permute-start | bytes 786440 | tf_op jit(solution)/shard_map/ppermute | solution.py:239
  113.5 0.7 copy-start.6
Sparse Core Ops, SparseCore 0:
  10.5 75.9 all-gather.1
